TPU v7x, 32 devices: a whole 2x2x4 slice. The times are simulated.
32 devices in a mesh: feat: 8 (over y, x, core), node: 4 (over z).
Axes of the slice: x: 2, y: 2, z: 4, core: 2. Of those that a mesh axis runs over, the one named last changes fastest.
Arguments:
- features: bfloat16 [4, 512, 16384], P('node', 'feat'), may hold values from -6 to 6
- target_ids: int32 [4, 4096], P('node'), may hold values from 0 to 16383
- block_ids: int32 [4, 32, 8], P('node'), may hold values from 0 to 127
- tile_counts: int32 [4, 32], P('node'), may hold values from 1 to 8, as said below
- adjacency: bfloat16 [4, 32, 8, 128, 128], P('node'), may hold values from 0 to 0.25
- w_neigh: bfloat16 [256, 512], P(None, 'feat'), may hold values from -0.1875 to 0.1875
- w_self: bfloat16 [256, 512], P(None, 'feat'), may hold values from -0.1875 to 0.1875
- w_head: bfloat16 [256, 256], replicated, may hold values from -0.375 to 0.375
- grad_scores: bfloat16 [4, 4096, 256], P('node', 'feat'), may hold values from -6 to 6
Outputs:
- scores: bfloat16 [4, 4096, 256], P('node', 'feat')
- grad_head: float32 [256, 256], replicated
- grad_neigh: float32 [256, 512], P(None, 'feat')
- grad_self: float32 [256, 512], P(None, 'feat')
Inputs may be any that keep to these rules, and one draw needn't show every extreme that they name: `tile_counts`: one group, drawn from the seed, has all of its tiles at 8 live slots; every tile of the other groups has fewer than 8.
All inputs are finite; a program needn't handle non-finite values.
Results may differ from a plain program's by a relative error of at most 0.0056.
Values may be sent and summed in bfloat16 or wider, within the bound.
A program may use at most 64 MiB of HBM per device.

v0:
```python
import jax
import jax.numpy as jnp
from jax import lax
from jax.sharding import PartitionSpec as P


def aggregate_local(feature_rows, block_row, count_row, adjacency_group):
    width = feature_rows.shape[0]
    tiles = block_row.shape[0]
    slots = block_row.shape[1]
    blocks = feature_rows.reshape(width, -1, 128)
    gathered = jnp.take(blocks, block_row.reshape(-1), axis=1).reshape(width, tiles, slots, 128)
    live = (jnp.arange(slots, dtype=jnp.int32)[None, :] < count_row[:, None]).astype(jnp.bfloat16)
    masked = gathered * live[None, :, :, None]
    summed = jnp.einsum(
        "tkrs,ftks->ftr", adjacency_group, masked, preferred_element_type=jnp.float32
    )
    summed = summed / count_row.astype(jnp.float32)[None, :, None]
    return summed.astype(jnp.bfloat16).reshape(width, tiles * 128)


def contract_first(left, right):
    return lax.dot_general(
        left, right, (((0,), (1,)), ((), ())), preferred_element_type=jnp.float32
    )


def body(
    features, target_ids, block_ids, tile_counts, adjacency, w_neigh, w_self, w_head, grad_scores
):
    feature_rows = features[0]
    aggregate = aggregate_local(feature_rows, block_ids[0], tile_counts[0], adjacency[0])
    own = jnp.take(feature_rows, target_ids[0], axis=1)
    agg_part = aggregate
    own_part = own
    preact = lax.psum_scatter(
        contract_first(agg_part, w_neigh) + contract_first(own_part, w_self),
        "feat",
        scatter_dimension=0,
        tiled=True,
    )
    hidden = jax.nn.silu(preact).astype(jnp.bfloat16)
    scores = jnp.dot(hidden, w_head.T, preferred_element_type=jnp.float32).astype(jnp.bfloat16)
    cotangent = grad_scores[0]
    head_local = lax.dot_general(
        cotangent, hidden, (((0,), (0,)), ((), ())), preferred_element_type=jnp.float32
    )
    grad_head = lax.psum(head_local, ("feat", "node"))
    grad_hidden = jnp.dot(cotangent, w_head, preferred_element_type=jnp.float32)
    sigma = jax.nn.sigmoid(preact)
    grad_pre = (grad_hidden * sigma * (1.0 + preact * (1.0 - sigma))).astype(jnp.bfloat16)
    shard_piece = lax.all_gather(grad_pre, "feat", axis=0, tiled=True)
    agg_part = aggregate
    own_part = own
    neigh_local = contract_first(shard_piece, agg_part)
    self_local = contract_first(shard_piece, own_part)
    grad_neigh, grad_self = lax.psum((neigh_local, self_local), "node")
    return (scores[None], grad_head, grad_neigh, grad_self)


def solution(mesh):
    in_specs = (
        P("node", "feat", None),
        P("node", None),
        P("node", None, None),
        P("node", None),
        P("node", None, None, None, None),
        P(None, "feat"),
        P(None, "feat"),
        P(),
        P("node", "feat", None),
    )
    out_specs = (P("node", "feat", None), P(), P(None, "feat"), P(None, "feat"))
    return jax.shard_map(body, mesh=mesh, in_specs=in_specs, out_specs=out_specs, check_vma=False)
```

profile of v0, /device:TPU:0, one launch (start us, length us, event | category | flops | bytes accessed | tf_op | source)
XLA Modules:
  0.0 308.8 jit_solution(13335983999297234126)
XLA Ops:
  7.2 0.0 copy-start
  7.2 0.0 copy-start.1
  7.2 0.0 reduce-scatter.2.cloned.1.call-start
  7.2 0.8 compare_and_fusion.1
  8.1 0.8 copy.23
  8.8 0.7 bitcast_convert_fusion
  9.5 0.1 copy.22
  9.6 0.7 compare_select_fusion
  10.3 0.7 compare_and_fusion
  11.1 0.7 fusion.33
  11.8 0.1 reshape_squeeze.10
  11.9 4.8 %copy.26 = bf16[1,64,16384]{1,2,0:T(8,128)(2,1)} copy(bf16[1,64,16384]{2,1,0:T(8,128)(2,1)} %param.9) | data formatting | bytes 4194304 | tf_op args[0]
  16.7 0.0 copy-done.1
  16.7 0.6 copy.30
  17.3 1.4 copy.24
  18.6 3.1 gather_fusion
  21.7 0.0 copy-start.4
  21.7 13.8 %gather_fusion.1 = bf16[4096,64]{1,0:T(8,128)(2,1)S(1)} fusion(bf16[64,16384]{0,1:T(8,128)(2,1)} %bitcast.57, s32[4096]{0:T(1024)S(1)} %broadcast_clamp_fusion), kind=kCustom, calls=%fused_computation.1 | custom fusion | bytes 1064960 | tf_op jit(solution)/shard_map/jit(_take)/gather | solution.py:33
  35.5 0.0 copy-done.4
  35.5 0.0 copy-start.2
  35.5 1.5 fusion.29
  37.0 0.7 copy-done.2
  37.7 5.7 %fusion.19 = bf16[32,8,8,128]{3,2,1,0:T(8,128)(2,1)S(1)} fusion(bf16[1,32,8,128,128]{4,3,2,1,0:T(8,128)(2,1)} %param.13, bf16[64,32,8,128]{3,0,2,1:T(8,128)(2,1)S(1)} %bitcast.60, pred[32,8]{1,0:T(8,128)(4,1)S(1)} %copy.22, bf16[32,8]{1,0:T(8,128)(2,1)S(1)} %fusion.33, f32[32]{0:T(128)S(1)} %bitcast_convert_fusion), kind=kOutput, calls=%fused_computation.19 | convolution fusion | flops 541589504 | bytes 13108096 | tf_op jit(solution)/shard_map/tkrs,ftks->ftr/dot_general | solution.py:15
  43.4 0.0 copy-done.5
  43.4 2.7 convolution_add_fusion
  46.1 0.0 reduce-scatter.2.cloned.1.call-update
  46.1 0.0 all-gather.2.cloned.1.call-start
  46.2 54.1 %reduce-scatter.2.cloned.1.call-done = f32[512,256]{1,0:T(8,128)} async-done(((f32[4096,256]{1,0:T(8,128)}), f32[512,256]{1,0:T(8,128)}) %reduce-scatter.2.cloned.1.call-update) | async-done | bytes 524304 | tf_op jit(solution)/shard_map/reduce_scatter | solution.py:36
  100.3 0.0 copy-done
  100.3 0.0 copy-done.7
  100.3 2.0 fusion.13
  102.3 0.0 all-gather.2.cloned.1.call-update
  102.4 0.0 all-reduce.4.cloned.1.call-start
  102.4 2.1 convolution_bitcast_fusion
  104.5 0.0 all-reduce.4.cloned.1.call-update
  104.5 0.0 all-reduce.6.cloned.1.call-start
  104.6 26.3 %all-gather.2.cloned.1.call-done = bf16[4096,256]{1,0:T(8,128)(2,1)} async-done(((bf16[512,256]{1,0:T(8,128)(2,1)}), bf16[4096,256]{1,0:T(8,128)(2,1)}) %all-gather.2.cloned.1.call-update) | async-done | bytes 2097168 | tf_op jit(solution)/shard_map/all_gather | solution.py:52
  130.9 4.9 %fusion.30 = f32[256,64]{0,1:T(8,128)} fusion(bf16[4096,256]{1,0:T(8,128)(2,1)} %all-gather.2.cloned.1.call-done, bf16[4096,64]{1,0:T(8,128)(2,1)S(1)} %gather_fusion.1, pred[4096]{0:T(1024)(128)(4,1)S(1)} %compare_and_fusion), kind=kOutput, calls=%fused_computation.28 | convolution fusion | flops 134479872 | bytes 2691072 | tf_op jit(solution)/shard_map/dot_general | solution.py:23
  135.8 0.0 copy-done.3
  135.8 1.1 fusion.24
  136.9 0.0 all-reduce.6.cloned.1.call-update
  136.9 0.0 copy-done.6
  136.9 1.0 fusion.14
  137.9 124.9 %all-reduce.4.cloned.1.call-done = f32[256,256]{0,1:T(8,128)} async-done(((f32[256,256]{0,1:T(8,128)}), f32[256,256]{0,1:T(8,128)}) %all-reduce.4.cloned.1.call-update) | async-done | bytes 262160 | tf_op jit(solution)/shard_map/psum | solution.py:48
  262.9 1.8 copy.27
  264.6 34.7 %all-reduce.6.cloned.1.call-done = (f32[256,64]{0,1:T(8,128)}, f32[256,64]{0,1:T(8,128)}) async-done(((f32[256,64]{0,1:T(8,128)}, f32[256,64]{0,1:T(8,128)}), (f32[256,64]{0,1:T(8,128)}, f32[256,64]{0,1:T(8,128)})) %all-reduce.6.cloned.1.call-update) | async-done | bytes 131088 | tf_op jit(solution)/shard_map/psum | solution.py:57
  299.4 1.5 copy.42
  300.8 1.5 copy.43
  (7 shorter events, 0.0 us)
Async XLA Ops:
  7.2 93.1 %copy-start = (bf16[1,512,256]{2,1,0:T(8,128)(2,1)S(1)}, bf16[1,512,256]{2,1,0:T(8,128)(2,1)}, u32[]{:S(2)}) copy-start(bf16[1,512,256]{2,1,0:T(8,128)(2,1)} %param.17) | copy-start | bytes 786436
  7.2 9.5 %copy-start.1 = (bf16[1,64,16384]{2,1,0:T(8,128)(2,1)S(1)}, bf16[1,64,16384]{2,1,0:T(8,128)(2,1)}, u32[]{:S(2)}) copy-start(bf16[1,64,16384]{2,1,0:T(8,128)(2,1)} %param.9) | copy-start | bytes 6291460
  7.2 93.1 %reduce-scatter.2.cloned.1.call-start = ((), (), s32[]{:S(2)}) async-start(), calls=%async_computation.1 | async-start | bytes 4718592 | tf_op jit(solution)/shard_map/reduce_scatter | solution.py:36
  21.7 13.8 %copy-start.4 = (bf16[256,64]{0,1:T(8,128)(2,1)S(1)}, bf16[256,64]{0,1:T(8,128)(2,1)}, u32[]{:S(2)}) copy-start(bf16[256,64]{0,1:T(8,128)(2,1)} %param.15) | copy-start | bytes 98308
  35.5 2.2 copy-start.2
  37.7 5.7 %copy-start.5 = (bf16[256,64]{0,1:T(8,128)(2,1)S(1)}, bf16[256,64]{0,1:T(8,128)(2,1)}, u32[]{:S(2)}) copy-start(bf16[256,64]{0,1:T(8,128)(2,1)} %param.14) | copy-start | bytes 98308
  46.1 54.2 %copy-start.7 = (bf16[256,256]{1,0:T(8,128)(2,1)S(1)}, bf16[256,256]{1,0:T(8,128)(2,1)}, u32[]{:S(2)}) copy-start(bf16[256,256]{1,0:T(8,128)(2,1)} %param.16) | copy-start | bytes 393220
  46.1 84.7 %all-gather.2.cloned.1.call-start = ((), (), s32[]{:S(2)}) async-start(), calls=%async_computation.3 | async-start | bytes 2359296 | tf_op jit(solution)/shard_map/all_gather | solution.py:52
  102.4 160.5 %all-reduce.4.cloned.1.call-start = ((), (), s32[]{:S(2)}) async-start(), calls=%async_computation.2 | async-start | bytes 524288 | tf_op jit(solution)/shard_map/psum | solution.py:48
  104.5 32.5 %copy-start.6 = (f32[512,256]{1,0:T(8,128)S(1)}, f32[512,256]{1,0:T(8,128)}, u32[]{:S(2)}) copy-start(f32[512,256]{1,0:T(8,128)} %reduce-scatter.2.cloned.1.call-done) | copy-start | bytes 1572868
  104.5 194.9 %all-reduce.6.cloned.1.call-start = ((), (), s32[]{:S(2)}) async-start(), calls=%async_computation.4 | async-start | bytes 262144 | tf_op jit(solution)/shard_map/psum | solution.py:57
  130.8 4.9 %copy-start.3 = (bf16[4096,256]{1,0:T(8,128)(2,1)S(1)}, bf16[4096,256]{1,0:T(8,128)(2,1)}, u32[]{:S(2)}) copy-start(bf16[4096,256]{1,0:T(8,128)(2,1)} %all-gather.2.cloned.1.call-done) | copy-start | bytes 6291460
Sparse Core Ops, SparseCore 0:
  46.2 53.9 reduce-scatter.1
  102.9 27.8 all-gather.1
  137.8 124.9 all-reduce.3
  265.8 33.5 all-reduce.5
where the time goes:
time: 309 us
  waiting for transfers between devices  240 us (78%)
  local copies, waits for them, and re-layouts  30 us (10%)
  matrix products  21 us (7%)
  between operations  13.9 us (4%)
  other arithmetic  3.71 us (1%)
    psum x1, waiting for transfers between devices, body(): grad_head = lax.psum(head_local, ('feat', 'node'))  125 us
    reduce_scatter x1, waiting for transfers between devices, body(): lax.psum_scatter(contract_first(agg_part, w_neigh) + contract_first(own_p...  54.1 us
    psum x1, waiting for transfers between devices, body(): grad_neigh, grad_self = lax.psum((neigh_local, self_local), 'node')  34.7 us
    all_gather x1, waiting for transfers between devices, body(): shard_piece = lax.all_gather(grad_pre, 'feat', axis=0, tiled=True)  26.3 us
    gather x1, local copies, waits for them, and re-layouts, body(): own = jnp.take(feature_rows, target_ids[0], axis=1)  13.8 us
    unnamed x22, local copies, waits for them, and re-layouts  11.6 us
    dot_general x4, matrix products, contract_first(): lax.dot_general(left, right, (((0,), (1,)), ((), ())), preferred_element_...  10.2 us
  transfers between devices with their start and end apart: 4, of which 4 were waited for; matrix products, arithmetic and copies ran while one was open for 4% of the time, Pallas kernels for 0%

commit v1 on v0

v1 whole, which is shorter than its diff:
```python
import functools

import jax
import jax.numpy as jnp
from jax import lax
from jax.experimental import pallas as pl
from jax.experimental.pallas import tpu as pltpu
from jax.sharding import PartitionSpec as P

F32 = jnp.float32
BF16 = jnp.bfloat16
VMEM_BYTES = 56 * 1024 * 1024


def nn(left, right):
    return lax.dot_general(left, right, (((1,), (0,)), ((), ())), preferred_element_type=F32)


def nt(left, right):
    return lax.dot_general(left, right, (((1,), (1,)), ((), ())), preferred_element_type=F32)


def gather_kernel(
    ids_ref, blocks_ref, counts_ref, feat_ref, wn_ref, ws_ref, own_ref, near_ref, wt_ref, table, rows
):
    width, sources = feat_ref.shape
    parts, _, targets = own_ref.shape
    wt_ref[:width, :] = wn_ref[...].astype(F32).T.astype(BF16)
    wt_ref[width:, :] = ws_ref[...].astype(F32).T.astype(BF16)

    def fill(step, carry):
        for piece in range(4):
            at = pl.multiple_of((step * 4 + piece) * 128, 128)
            table[pl.ds(at, 128), :] = feat_ref[:, pl.ds(at, 128)].astype(F32).T
        return carry

    lax.fori_loop(0, sources // 512, fill, 0)

    tiles = near_ref.shape[0]
    slots = near_ref.shape[2] // 128

    def neighbours(tile, carry):
        count = counts_ref[tile]
        for slot in range(slots):
            at = pl.multiple_of(blocks_ref[tile * slots + slot] * 128, 128)
            live = jnp.full((width, 128), (slot < count).astype(F32), F32).astype(BF16)
            near_ref[tile, :, slot * 128 : slot * 128 + 128] = feat_ref[:, pl.ds(at, 128)] * live
        return carry

    lax.fori_loop(0, tiles, neighbours, 0)

    def chunk(step, carry):
        base = step * 128
        for row in range(128):
            rows[row : row + 1, :] = table[pl.ds(ids_ref[base + row], 1), :]
        part = base // targets
        inside = pl.multiple_of(base - part * targets, 128)
        own_ref[part, :, pl.ds(inside, 128)] = rows[...].T.astype(BF16)
        return carry

    lax.fori_loop(0, parts * targets // 128, chunk, 0)


def gather_own(ids, blocks, counts, feat, w_neigh, w_self, parts):
    width, sources = feat.shape
    hid = w_neigh.shape[0]
    targets = ids.shape[0] // parts
    tiles, slots = counts.shape[0], blocks.shape[0] // counts.shape[0]
    vmem = pl.BlockSpec(memory_space=pltpu.VMEM)
    smem = pl.BlockSpec(memory_space=pltpu.SMEM)
    return pl.pallas_call(
        gather_kernel,
        out_shape=(
            jax.ShapeDtypeStruct((parts, width, targets), BF16),
            jax.ShapeDtypeStruct((tiles, width, slots * 128), BF16),
            jax.ShapeDtypeStruct((2 * width, hid), BF16),
        ),
        in_specs=[smem, smem, smem, vmem, vmem, vmem],
        out_specs=(vmem, vmem, vmem),
        scratch_shapes=[pltpu.VMEM((sources, width), F32), pltpu.VMEM((128, width), F32)],
        compiler_params=pltpu.CompilerParams(vmem_limit_bytes=VMEM_BYTES),
        name="own_gather",
    )(ids, blocks, counts, feat, w_neigh, w_self)


def main_kernel(
    parts, nodes, counts_ref, near_ref, adj_ref, own_ref, wt_ref, wh_ref, gs_ref,
    scores_ref, grads_ref, head_ref,
    x_all, w_all, agg_send, head_part, head_recv, head_node, head_all,
    g_part, g_send, g_recv, g_node,
    w_sems, own_sems, agg_sems, hrs_sems, grs_sems, hn_sems, gn_sems, hag_sems,
):
    me = lax.axis_index("feat")
    my_node = lax.axis_index("node")
    width = near_ref.shape[1]
    tiles, slots = adj_ref.shape[:2]
    per_part = tiles // parts
    hid = wh_ref.shape[1]
    targets = gs_ref.shape[0]

    def feat_copy(step, src, dst, sems):
        peer = lax.rem(me + step, parts)
        return pltpu.make_async_remote_copy(
            src_ref=src, dst_ref=dst, send_sem=sems.at[0, step], recv_sem=sems.at[1, step],
            device_id={"feat": peer}, device_id_type=pl.DeviceIdType.MESH,
        )

    def node_copy(step, src, dst, sems):
        peer = lax.rem(my_node + step, nodes)
        return pltpu.make_async_remote_copy(
            src_ref=src, dst_ref=dst, send_sem=sems.at[0, step], recv_sem=sems.at[1, step],
            device_id={"node": peer}, device_id_type=pl.DeviceIdType.MESH,
        )

    barrier = pltpu.get_barrier_semaphore()
    for step in range(1, parts):
        pl.semaphore_signal(
            barrier, inc=1, device_id={"feat": lax.rem(me + step, parts)},
            device_id_type=pl.DeviceIdType.MESH,
        )
    for step in range(1, nodes):
        pl.semaphore_signal(
            barrier, inc=1, device_id={"node": lax.rem(my_node + step, nodes)},
            device_id_type=pl.DeviceIdType.MESH,
        )
    pl.semaphore_wait(barrier, parts + nodes - 2)

    w_copies, own_copies, agg_copies = [], [], []
    for step in range(1, parts):
        peer = lax.rem(me + step, parts)
        copy = feat_copy(step, own_ref.at[peer], x_all.at[me, pl.ds(width, width)], own_sems)
        copy.start()
        own_copies.append(copy)
        copy = feat_copy(step, wt_ref, w_all.at[me], w_sems)
        copy.start()
        w_copies.append(copy)

    def aggregate(tile):
        edges = jnp.concatenate([adj_ref[tile, slot] for slot in range(slots)], axis=1)
        total = nt(near_ref[tile], edges)
        return (total / jnp.full(total.shape, counts_ref[tile], F32)).astype(BF16)

    for step in range(1, parts + 1):
        peer = lax.rem(me + step, parts)
        for tile in range(per_part):
            part = aggregate(peer * per_part + tile)
            if step < parts:
                agg_send[step, :, tile * 128 : tile * 128 + 128] = part
            else:
                x_all[me, :width, tile * 128 : tile * 128 + 128] = part
        if step < parts:
            copy = feat_copy(step, agg_send.at[step], x_all.at[me, pl.ds(0, width)], agg_sems)
            copy.start()
            agg_copies.append(copy)
    x_all[me, width:, :] = own_ref[me]
    w_all[me] = wt_ref[...]

    grad_t = gs_ref[...].astype(F32).T.astype(BF16)
    head_t = wh_ref[...].astype(F32).T.astype(BF16)
    grad_hidden = nn(head_t, grad_t)

    for copy in w_copies:
        copy.wait_recv()
    weights = w_all[...].reshape(parts * 2 * width, hid).astype(F32).T.astype(BF16)
    for copy in own_copies:
        copy.wait_recv()
    for copy in agg_copies:
        copy.wait_recv()
    x = x_all[...].reshape(parts * 2 * width, targets)
    preact = nn(weights, x)
    sigma = 1.0 / (1.0 + jnp.exp(-preact))
    hidden = (preact * sigma).astype(BF16)
    head_part[...] = nt(grad_t, hidden).reshape(head_part.shape)
    hrs = []
    for step in range(1, parts):
        peer = lax.rem(me + step, parts)
        copy = feat_copy(step, head_part.at[peer], head_recv.at[step], hrs_sems)
        copy.start()
        hrs.append(copy)
    grad_pre = (grad_hidden * sigma * (1.0 + preact * (1.0 - sigma))).astype(BF16)
    grads = nt(x, grad_pre).reshape(g_part.shape)
    g_part[...] = grads
    g_send[...] = grads.astype(BF16)
    grs = []
    for step in range(1, parts):
        peer = lax.rem(me + step, parts)
        copy = feat_copy(step, g_send.at[peer], g_recv.at[step], grs_sems)
        copy.start()
        grs.append(copy)
    scores_ref[...] = nn(wh_ref[...], hidden).T.astype(BF16)

    total = head_part[me]
    for step, copy in enumerate(hrs, 1):
        copy.wait_recv()
        total += head_recv[step]
    head_node[my_node] = total
    hns = []
    for step in range(1, nodes):
        copy = node_copy(step, head_node.at[my_node], head_node.at[my_node], hn_sems)
        copy.start()
        hns.append(copy)

    total = g_part[me]
    for step, copy in enumerate(grs, 1):
        copy.wait_recv()
        total += g_recv[step].astype(F32)
    g_node[my_node] = total.astype(BF16)
    gns = []
    for step in range(1, nodes):
        copy = node_copy(step, g_node.at[my_node], g_node.at[my_node], gn_sems)
        copy.start()
        gns.append(copy)

    for copy in hns:
        copy.wait_recv()
    total = head_node[0]
    for node in range(1, nodes):
        total += head_node[node]
    head_all[me] = total
    hags = []
    for step in range(1, parts):
        copy = feat_copy(step, head_all.at[me], head_all.at[me], hag_sems)
        copy.start()
        hags.append(copy)

    for copy in gns:
        copy.wait_recv()
    total = g_node[0].astype(F32)
    for node in range(1, nodes):
        total += g_node[node].astype(F32)
    grads_ref[...] = total

    for copy in hags:
        copy.wait_recv()
    head_ref[...] = head_all[...].reshape(head_ref.shape)
    for copy in (*w_copies, *own_copies, *agg_copies, *hrs, *grs, *hns, *gns, *hags):
        copy.wait_send()


def main_call(parts, nodes, counts, near, adj, own, wt, w_head, grad_scores):
    width = near.shape[1]
    targets, out = grad_scores.shape
    hid = w_head.shape[1]
    vmem = pl.BlockSpec(memory_space=pltpu.VMEM)
    smem = pl.BlockSpec(memory_space=pltpu.SMEM)
    head_rows = out // parts
    feat_sems = pltpu.SemaphoreType.DMA((2, parts))
    node_sems = pltpu.SemaphoreType.DMA((2, nodes))
    return pl.pallas_call(
        functools.partial(main_kernel, parts, nodes),
        out_shape=(
            jax.ShapeDtypeStruct((targets, out), BF16),
            jax.ShapeDtypeStruct((2 * width, hid), F32),
            jax.ShapeDtypeStruct((out, hid), F32),
        ),
        in_specs=[smem] + [vmem] * 6,
        out_specs=(vmem, vmem, vmem),
        scratch_shapes=[
            pltpu.VMEM((parts, 2 * width, targets), BF16),
            pltpu.VMEM((parts, 2 * width, hid), BF16),
            pltpu.VMEM((parts, width, targets), BF16),
            pltpu.VMEM((parts, head_rows, hid), F32),
            pltpu.VMEM((parts, head_rows, hid), F32),
            pltpu.VMEM((nodes, head_rows, hid), F32),
            pltpu.VMEM((parts, head_rows, hid), F32),
            pltpu.VMEM((parts, 2 * width, hid), F32),
            pltpu.VMEM((parts, 2 * width, hid), BF16),
            pltpu.VMEM((parts, 2 * width, hid), BF16),
            pltpu.VMEM((nodes, 2 * width, hid), BF16),
            feat_sems, feat_sems, feat_sems, feat_sems, feat_sems, node_sems, node_sems, feat_sems,
        ],
        compiler_params=pltpu.CompilerParams(
            collective_id=0, has_side_effects=True, vmem_limit_bytes=VMEM_BYTES
        ),
        name="train_step",
    )(counts, near, adj, own, wt, w_head, grad_scores)


def solution(mesh):
    parts, nodes = mesh.shape["feat"], mesh.shape["node"]

    def body(
        features, target_ids, block_ids, tile_counts, adjacency, w_neigh, w_self, w_head, grad_scores
    ):
        feat = features[0]
        width = feat.shape[0]
        counts = tile_counts[0]
        own, near, wt = gather_own(
            target_ids[0], block_ids[0].reshape(-1), counts, feat, w_neigh, w_self, parts
        )
        scores, grads, head = main_call(
            parts, nodes, counts.astype(F32), near, adjacency[0], own, wt, w_head, grad_scores[0]
        )
        return scores[None], head, grads[:width].T, grads[width:].T

    in_specs = (
        P("node", "feat", None),
        P("node", None),
        P("node", None, None),
        P("node", None),
        P("node", None, None, None, None),
        P(None, "feat"),
        P(None, "feat"),
        P(),
        P("node", "feat", None),
    )
    out_specs = (P("node", "feat", None), P(), P(None, "feat"), P(None, "feat"))
    return jax.shard_map(body, mesh=mesh, in_specs=in_specs, out_specs=out_specs, check_vma=False)
```

time: 309 us -> 73.5 us (0.24)
  waiting for transfers between devices: 240 us -> 0 us
  Pallas kernels: 0 us -> 61.1 us
  matrix products: 21 us -> 0 us
  local copies, waits for them, and re-layouts: 30 us -> 9.26 us
  between operations: 13.9 us -> 0.64 us
    psum x2 -> x0, waiting for transfers between devices: 160 us -> none  [the longest x1 125 us: body(): grad_head = lax.psum(head_local, ('feat', 'node'))]
    pallas_call x0 -> x2, Pallas kernels: none -> 61.1 us  [the longest x1 46.7 us: main_call(): pl.pallas_call(functools.partial(main_kernel, parts, nodes), out_shape=(j...]
    reduce_scatter x1 -> x0, waiting for transfers between devices: 54.1 us -> none  [body(): lax.psum_scatter(contract_first(agg_part, w_neigh) + contract_first(own_p...]
    all_gather x1 -> x0, waiting for transfers between devices: 26.3 us -> none  [body(): shard_piece = lax.all_gather(grad_pre, 'feat', axis=0, tiled=True)]
    dot_general x8 -> x0, matrix products: 21 us -> none  [the longest x4 10.2 us: contract_first(): lax.dot_general(left, right, (((0,), (1,)), ((), ())), preferred_element_...]
    gather x2 -> x0, local copies, waits for them, and re-layouts: 16.9 us -> none  [the longest x1 13.8 us: body(): own = jnp.take(feature_rows, target_ids[0], axis=1)]
    unnamed x22 -> x5, local copies, waits for them, and re-layouts: 11.6 us -> 7.08 us
  transfers between devices with their start and end apart: 4 -> 0, of which waited for: 4 -> 0; matrix products, arithmetic and copies ran while one was open for 4% -> 0% of each run, Pallas kernels for 0% -> 0%
where the time goes in v1:
time: 73.5 us; the launch traced here: 72.3 us
  Pallas kernels  61.1 us (83%)
  local copies, waits for them, and re-layouts  9.26 us (13%)
  other arithmetic  1.23 us (2%)
    pallas_call x1, Pallas kernels, main_call(): pl.pallas_call(functools.partial(main_kernel, parts, nodes), out_shape=(j...  46.7 us
    pallas_call x1, Pallas kernels, gather_own(): pl.pallas_call(gather_kernel, out_shape=(jax.ShapeDtypeStruct((parts, wid...  14.5 us
    unnamed x5, local copies, waits for them, and re-layouts  7.08 us
    transpose x1, local copies, waits for them, and re-layouts, body(): return (scores[None], head, grads[:width].T, grads[width:].T)  1.53 us

profile of v1, /device:TPU:0, one launch (start us, length us, event | category | flops | bytes accessed | tf_op | source)
XLA Modules:
  0.0 72.3 jit_solution(5212937886016680853)
XLA Ops:
  0.6 1.2 %bitcast_convert_fusion.counts_ref = f32[32]{0:T(128)} fusion(s32[1,32]{1,0:T(1,128)} %param.12), kind=kLoop, calls=%fused_computation.2 | loop fusion | flops 32 | bytes 256 | tf_op jit(solution)/shard_map/convert_element_type | solution.py:292
  1.9 0.8 %copy.15 = s32[1,32,8]{2,1,0:T(8,128)S(1)} copy(s32[1,32,8]{1,2,0:T(8,128)} %param.11) | data formatting | bytes 2048 | tf_op args[2]
  2.6 0.7 reshape_squeeze.3.blocks_ref
  3.3 1.5 %copy.16.wn_ref = bf16[256,64]{1,0:T(8,128)(2,1)} copy(bf16[256,64]{0,1:T(8,128)(2,1)} %param.14) | data formatting | bytes 65536 | tf_op args[5]
  4.8 1.5 %copy.17.ws_ref = bf16[256,64]{1,0:T(8,128)(2,1)} copy(bf16[256,64]{0,1:T(8,128)(2,1)} %param.15) | data formatting | bytes 65536 | tf_op args[6]
  6.3 14.5 %own_gather.1 = (bf16[8,64,512]{2,1,0:T(8,128)(2,1)}, bf16[32,64,1024]{2,1,0:T(8,128)(2,1)}, bf16[128,256]{1,0:T(8,128)(2,1)}) custom-call(s32[4096]{0:T(1024)} %bitcast.15, s32[256]{0:T(256)} %reshape_squeeze.3.blocks_ref, s32[32]{0:T(128)} %bitcast.16, bf16[64,16384]{1,0:T(8,128)(2,1)} %bitcast.12, bf16[256,64]{1,0:T(8,128)(2,1)} %copy.16.wn_ref, ...), custom_call_target="tpu_custom_call" | custom-call | tf_op jit(solution)/shard_map/own_gather/pallas_call | solution.py:71
  20.7 46.7 %train_step.1 = (bf16[512,256]{1,0:T(8,128)(2,1)}, f32[128,256]{1,0:T(8,128)}, f32[256,256]{1,0:T(8,128)}) custom-call(f32[32]{0:T(128)} %bitcast_convert_fusion.counts_ref, bf16[32,64,1024]{2,1,0:T(8,128)(2,1)} %get-tuple-element.10.near_ref, bf16[32,8,128,128]{3,2,1,0:T(8,128)(2,1)} %bitcast.11, bf16[8,64,512]{2,1,0:T(8,128)(2,1)} %get-tuple-element.11.own_ref, ...), custom_call_target="tpu_custom_call" | custom-call | tf_op jit(solution)/shard_map/train_step/pallas_call | solution.py:249
  67.4 1.5 %slice_bitcast_fusion = (f32[256,64]{0,1:T(8,128)}, f32[256,64]{0,1:T(8,128)}) fusion(f32[128,256]{1,0:T(8,128)} %get-tuple-element.15), kind=kLoop, calls=%fused_computation | loop fusion | bytes 262144 | tf_op jit(solution)/shard_map/transpose | solution.py:294
  68.9 1.7 %copy.20 = bf16[1,512,256]{2,1,0:T(8,128)(2,1)} copy(bf16[1,512,256]{2,1,0:T(8,128)(2,1)} %bitcast.13) | data formatting | bytes 524288
  70.6 1.7 %copy.21 = f32[256,256]{1,0:T(8,128)} copy(f32[256,256]{1,0:T(8,128)} %get-tuple-element.23) | data formatting | bytes 524288

commit v2 on v1

--- a/solution.py
+++ b/solution.py
@@ -21,12 +21,29 @@
 
 
 def gather_kernel(
-    ids_ref, blocks_ref, counts_ref, feat_ref, wn_ref, ws_ref, own_ref, near_ref, wt_ref, table, rows
+    ids_ref, blocks_ref, counts_ref, feat_ref, wn_ref, ws_ref, own_ref, near_out, wt_ref, inv_ref,
+    table, rows, near_ref, near_sem,
 ):
     width, sources = feat_ref.shape
     parts, _, targets = own_ref.shape
-    wt_ref[:width, :] = wn_ref[...].astype(F32).T.astype(BF16)
-    wt_ref[width:, :] = ws_ref[...].astype(F32).T.astype(BF16)
+    wt_ref[:width, :] = wn_ref[...]
+    wt_ref[width:, :] = ws_ref[...]
+
+    tiles = near_ref.shape[0]
+    slots = near_ref.shape[2] // 128
+
+    def neighbours(tile, carry):
+        count = counts_ref[tile]
+        inv_ref[pl.ds(tile, 1), :] = 1.0 / jnp.full((1, 128), count.astype(F32), F32)
+        for slot in range(slots):
+            at = pl.multiple_of(blocks_ref[slot, tile] * 128, 128)
+            live = jnp.full((width, 128), (slot < count).astype(F32), F32).astype(BF16)
+            near_ref[tile, :, slot * 128 : slot * 128 + 128] = feat_ref[:, pl.ds(at, 128)] * live
+        return carry
+
+    lax.fori_loop(0, tiles, neighbours, 0)
+    near_copy = pltpu.make_async_copy(near_ref, near_out, near_sem)
+    near_copy.start()
 
     def fill(step, carry):
         for piece in range(4):
@@ -35,19 +52,6 @@
         return carry
 
     lax.fori_loop(0, sources // 512, fill, 0)
-
-    tiles = near_ref.shape[0]
-    slots = near_ref.shape[2] // 128
-
-    def neighbours(tile, carry):
-        count = counts_ref[tile]
-        for slot in range(slots):
-            at = pl.multiple_of(blocks_ref[tile * slots + slot] * 128, 128)
-            live = jnp.full((width, 128), (slot < count).astype(F32), F32).astype(BF16)
-            near_ref[tile, :, slot * 128 : slot * 128 + 128] = feat_ref[:, pl.ds(at, 128)] * live
-        return carry
-
-    lax.fori_loop(0, tiles, neighbours, 0)
 
     def chunk(step, carry):
         base = step * 128
@@ -59,13 +63,14 @@
         return carry
 
     lax.fori_loop(0, parts * targets // 128, chunk, 0)
+    near_copy.wait()
 
 
 def gather_own(ids, blocks, counts, feat, w_neigh, w_self, parts):
     width, sources = feat.shape
-    hid = w_neigh.shape[0]
+    hid = w_neigh.shape[1]
     targets = ids.shape[0] // parts
-    tiles, slots = counts.shape[0], blocks.shape[0] // counts.shape[0]
+    slots, tiles = blocks.shape
     vmem = pl.BlockSpec(memory_space=pltpu.VMEM)
     smem = pl.BlockSpec(memory_space=pltpu.SMEM)
     return pl.pallas_call(
@@ -74,21 +79,28 @@
             jax.ShapeDtypeStruct((parts, width, targets), BF16),
             jax.ShapeDtypeStruct((tiles, width, slots * 128), BF16),
             jax.ShapeDtypeStruct((2 * width, hid), BF16),
+            jax.ShapeDtypeStruct((tiles, 128), F32),
         ),
         in_specs=[smem, smem, smem, vmem, vmem, vmem],
-        out_specs=(vmem, vmem, vmem),
-        scratch_shapes=[pltpu.VMEM((sources, width), F32), pltpu.VMEM((128, width), F32)],
+        out_specs=(vmem, pl.BlockSpec(memory_space=pl.ANY), vmem, vmem),
+        scratch_shapes=[
+            pltpu.VMEM((sources, width), F32),
+            pltpu.VMEM((128, width), F32),
+            pltpu.VMEM((tiles, width, slots * 128), BF16),
+            pltpu.SemaphoreType.DMA,
+        ],
         compiler_params=pltpu.CompilerParams(vmem_limit_bytes=VMEM_BYTES),
         name="own_gather",
     )(ids, blocks, counts, feat, w_neigh, w_self)
 
 
 def main_kernel(
-    parts, nodes, counts_ref, near_ref, adj_ref, own_ref, wt_ref, wh_ref, gs_ref,
+    parts, nodes, inv_ref, near_hbm, adj_hbm, own_ref, wt_ref, wh_ref, gs_ref,
     scores_ref, grads_ref, head_ref,
-    x_all, w_all, agg_send, head_part, head_recv, head_node, head_all,
+    near_ref, adj_ref, x_all, w_all, agg_send, head_part, head_recv, head_node, head_all,
     g_part, g_send, g_recv, g_node,
     w_sems, own_sems, agg_sems, hrs_sems, grs_sems, hn_sems, gn_sems, hag_sems,
+    load_sems,
 ):
     me = lax.axis_index("feat")
     my_node = lax.axis_index("node")
@@ -112,6 +124,18 @@
             device_id={"node": peer}, device_id_type=pl.DeviceIdType.MESH,
         )
 
+    loads = []
+    for step in range(1, parts + 1):
+        first = lax.rem(me + step, parts) * per_part
+        for which, (src, dst) in enumerate(((near_hbm, near_ref), (adj_hbm, adj_ref))):
+            copy = pltpu.make_async_copy(
+                src.at[pl.ds(first, per_part)],
+                dst.at[pl.ds((step - 1) * per_part, per_part)],
+                load_sems.at[which, step - 1],
+            )
+            copy.start()
+            loads.append(copy)
+
     barrier = pltpu.get_barrier_semaphore()
     for step in range(1, parts):
         pl.semaphore_signal(
@@ -135,15 +159,16 @@
         copy.start()
         w_copies.append(copy)
 
-    def aggregate(tile):
-        edges = jnp.concatenate([adj_ref[tile, slot] for slot in range(slots)], axis=1)
-        total = nt(near_ref[tile], edges)
-        return (total / jnp.full(total.shape, counts_ref[tile], F32)).astype(BF16)
+    def aggregate(held, tile):
+        edges = jnp.concatenate([adj_ref[held, slot] for slot in range(slots)], axis=1)
+        return (nt(near_ref[held], edges) * inv_ref[pl.ds(tile, 1), :]).astype(BF16)
 
     for step in range(1, parts + 1):
         peer = lax.rem(me + step, parts)
+        loads[2 * step - 2].wait()
+        loads[2 * step - 1].wait()
         for tile in range(per_part):
-            part = aggregate(peer * per_part + tile)
+            part = aggregate((step - 1) * per_part + tile, peer * per_part + tile)
             if step < parts:
                 agg_send[step, :, tile * 128 : tile * 128 + 128] = part
             else:
@@ -237,12 +262,12 @@
         copy.wait_send()
 
 
-def main_call(parts, nodes, counts, near, adj, own, wt, w_head, grad_scores):
+def main_call(parts, nodes, inv, near, adj, own, wt, w_head, grad_scores):
     width = near.shape[1]
     targets, out = grad_scores.shape
     hid = w_head.shape[1]
     vmem = pl.BlockSpec(memory_space=pltpu.VMEM)
-    smem = pl.BlockSpec(memory_space=pltpu.SMEM)
+    anywhere = pl.BlockSpec(memory_space=pl.ANY)
     head_rows = out // parts
     feat_sems = pltpu.SemaphoreType.DMA((2, parts))
     node_sems = pltpu.SemaphoreType.DMA((2, nodes))
@@ -253,9 +278,11 @@
             jax.ShapeDtypeStruct((2 * width, hid), F32),
             jax.ShapeDtypeStruct((out, hid), F32),
         ),
-        in_specs=[smem] + [vmem] * 6,
+        in_specs=[vmem, anywhere, anywhere] + [vmem] * 4,
         out_specs=(vmem, vmem, vmem),
         scratch_shapes=[
+            pltpu.VMEM(near.shape, BF16),
+            pltpu.VMEM(adj.shape, BF16),
             pltpu.VMEM((parts, 2 * width, targets), BF16),
             pltpu.VMEM((parts, 2 * width, hid), BF16),
             pltpu.VMEM((parts, width, targets), BF16),
@@ -268,12 +295,35 @@
             pltpu.VMEM((parts, 2 * width, hid), BF16),
             pltpu.VMEM((nodes, 2 * width, hid), BF16),
             feat_sems, feat_sems, feat_sems, feat_sems, feat_sems, node_sems, node_sems, feat_sems,
+            pltpu.SemaphoreType.DMA((2, parts)),
         ],
         compiler_params=pltpu.CompilerParams(
             collective_id=0, has_side_effects=True, vmem_limit_bytes=VMEM_BYTES
         ),
         name="train_step",
-    )(counts, near, adj, own, wt, w_head, grad_scores)
+    )(inv, near, adj, own, wt, w_head, grad_scores)
+
+
+def hand_over_kernel(scores_in, head_in, grads_in, scores_ref, head_ref, neigh_ref, self_ref):
+    width = neigh_ref.shape[0]
+    scores_ref[...] = scores_in[...]
+    head_ref[...] = head_in[...]
+    neigh_ref[...] = grads_in[:width, :]
+    self_ref[...] = grads_in[width:, :]
+
+
+def hand_over(scores, head, grads):
+    vmem = pl.BlockSpec(memory_space=pltpu.VMEM)
+    half = jax.ShapeDtypeStruct((grads.shape[0] // 2, grads.shape[1]), F32)
+    return pl.pallas_call(
+        hand_over_kernel,
+        out_shape=(
+            jax.ShapeDtypeStruct(scores.shape, BF16), jax.ShapeDtypeStruct(head.shape, F32), half, half,
+        ),
+        in_specs=[vmem] * 3,
+        out_specs=(vmem,) * 4,
+        name="hand_over",
+    )(scores, head, grads)
 
 
 def solution(mesh):
@@ -283,15 +333,15 @@
         features, target_ids, block_ids, tile_counts, adjacency, w_neigh, w_self, w_head, grad_scores
     ):
         feat = features[0]
-        width = feat.shape[0]
         counts = tile_counts[0]
-        own, near, wt = gather_own(
-            target_ids[0], block_ids[0].reshape(-1), counts, feat, w_neigh, w_self, parts
+        own, near, wt, inv = gather_own(
+            target_ids[0], block_ids[0].T, counts, feat, w_neigh.T, w_self.T, parts
         )
         scores, grads, head = main_call(
-            parts, nodes, counts.astype(F32), near, adjacency[0], own, wt, w_head, grad_scores[0]
-        )
-        return scores[None], head, grads[:width].T, grads[width:].T
+            parts, nodes, inv, near, adjacency[0], own, wt, w_head, grad_scores[0]
+        )
+        scores, head, neigh, own_grad = hand_over(scores, head, grads)
+        return scores[None], head, neigh.T, own_grad.T
 
     in_specs = (
         P("node", "feat", None),

time: 73.5 us -> 59.8 us (0.81)
  local copies, waits for them, and re-layouts: 9.26 us -> 0 us
  Pallas kernels: 61.1 us -> 58.2 us
  other arithmetic: 1.23 us -> 0 us
    unnamed x5 -> x0, local copies, waits for them, and re-layouts: 7.08 us -> none
    pallas_call x1, Pallas kernels: 46.7 us -> 43.2 us  [main_call(): pl.pallas_call(functools.partial(main_kernel, parts, nodes), out_shape=(j...]
    pallas_call x0 -> x1, Pallas kernels: none -> 1.91 us  [hand_over(): pl.pallas_call(hand_over_kernel, out_shape=(jax.ShapeDtypeStruct(scores.s...]
    transpose x1 -> x0, local copies, waits for them, and re-layouts: 1.53 us -> none  [body(): return (scores[None], head, grads[:width].T, grads[width:].T)]
    pallas_call x1, Pallas kernels: 14.5 us -> 13.1 us  [gather_own(): pl.pallas_call(gather_kernel, out_shape=(jax.ShapeDtypeStruct((parts, wid...]
    convert_element_type x1 -> x0, other arithmetic: 1.23 us -> none  [body(): counts.astype(F32)]
where the time goes in v2:
time: 59.8 us; the launch traced here: 58.8 us
  Pallas kernels  58.2 us (97%)
  between operations  0.65 us (1%)
    pallas_call x1, Pallas kernels, main_call(): pl.pallas_call(functools.partial(main_kernel, parts, nodes), out_shape=(j...  43.2 us
    pallas_call x1, Pallas kernels, gather_own(): pl.pallas_call(gather_kernel, out_shape=(jax.ShapeDtypeStruct((parts, wid...  13.1 us
    pallas_call x1, Pallas kernels, hand_over(): pl.pallas_call(hand_over_kernel, out_shape=(jax.ShapeDtypeStruct(scores.s...  1.91 us

profile of v2, /device:TPU:0, one launch (start us, length us, event | category | flops | bytes accessed | tf_op | source)
XLA Modules:
  0.0 58.8 jit_solution(8413902396984731171)
XLA Ops:
  0.6 13.1 %own_gather.1 = (bf16[8,64,512]{2,1,0:T(8,128)(2,1)}, bf16[32,64,1024]{2,1,0:T(8,128)(2,1)}, bf16[128,256]{1,0:T(8,128)(2,1)}, f32[32,128]{1,0:T(8,128)}) custom-call(s32[4096]{0:T(1024)} %bitcast.18, s32[8,32]{1,0:T(8,128)} %bitcast.19, s32[32]{0:T(128)} %bitcast.20, bf16[64,16384]{1,0:T(8,128)(2,1)} %bitcast.14, bf16[64,256]{1,0:T(8,128)(2,1)} %bitcast.16, ...), custom_call_target="tpu_custom_call" | custom-call | tf_op jit(solution)/shard_map/own_gather/pallas_call | solution.py:76
  13.7 43.2 %train_step.1 = (bf16[512,256]{1,0:T(8,128)(2,1)}, f32[128,256]{1,0:T(8,128)}, f32[256,256]{1,0:T(8,128)}) custom-call(f32[32,128]{1,0:T(8,128)} %get-tuple-element.15.inv_ref, bf16[32,64,1024]{2,1,0:T(8,128)(2,1)} %get-tuple-element.16.near_hbm, bf16[32,8,128,128]{3,2,1,0:T(8,128)(2,1)} %bitcast.13, bf16[8,64,512]{2,1,0:T(8,128)(2,1)} %get-tuple-element.17.own_ref, ...), custom_call_target="tpu_custom_call" | custom-call | tf_op jit(solution)/shard_map/train_step/pallas_call | solution.py:274
  56.9 1.9 %hand_over.1 = (bf16[512,256]{1,0:T(8,128)(2,1)}, f32[256,256]{1,0:T(8,128)}, f32[64,256]{1,0:T(8,128)}, f32[64,256]{1,0:T(8,128)}) custom-call(bf16[512,256]{1,0:T(8,128)(2,1)} %get-tuple-element.19.scores_in, f32[256,256]{1,0:T(8,128)} %get-tuple-element.20.head_in, f32[128,256]{1,0:T(8,128)} %get-tuple-element.21.grads_in), custom_call_target="tpu_custom_call" | custom-call | tf_op jit(solution)/shard_map/hand_over/pallas_call | solution.py:318

commit v3 on v2

--- a/solution.py
+++ b/solution.py
@@ -21,14 +21,11 @@
 
 
 def gather_kernel(
-    ids_ref, blocks_ref, counts_ref, feat_ref, wn_ref, ws_ref, own_ref, near_out, wt_ref, inv_ref,
+    ids_ref, blocks_ref, counts_ref, feat_ref, own_ref, near_out, inv_ref,
     table, rows, near_ref, near_sem,
 ):
     width, sources = feat_ref.shape
     parts, _, targets = own_ref.shape
-    wt_ref[:width, :] = wn_ref[...]
-    wt_ref[width:, :] = ws_ref[...]
-
     tiles = near_ref.shape[0]
     slots = near_ref.shape[2] // 128
 
@@ -66,9 +63,8 @@
     near_copy.wait()
 
 
-def gather_own(ids, blocks, counts, feat, w_neigh, w_self, parts):
+def gather_own(ids, blocks, counts, feat, parts):
     width, sources = feat.shape
-    hid = w_neigh.shape[1]
     targets = ids.shape[0] // parts
     slots, tiles = blocks.shape
     vmem = pl.BlockSpec(memory_space=pltpu.VMEM)
@@ -78,11 +74,10 @@
         out_shape=(
             jax.ShapeDtypeStruct((parts, width, targets), BF16),
             jax.ShapeDtypeStruct((tiles, width, slots * 128), BF16),
-            jax.ShapeDtypeStruct((2 * width, hid), BF16),
             jax.ShapeDtypeStruct((tiles, 128), F32),
         ),
-        in_specs=[smem, smem, smem, vmem, vmem, vmem],
-        out_specs=(vmem, pl.BlockSpec(memory_space=pl.ANY), vmem, vmem),
+        in_specs=[smem, smem, smem, vmem],
+        out_specs=(vmem, pl.BlockSpec(memory_space=pl.ANY), vmem),
         scratch_shapes=[
             pltpu.VMEM((sources, width), F32),
             pltpu.VMEM((128, width), F32),
@@ -90,16 +85,17 @@
             pltpu.SemaphoreType.DMA,
         ],
         compiler_params=pltpu.CompilerParams(vmem_limit_bytes=VMEM_BYTES),
+        cost_estimate=pl.CostEstimate(flops=0, bytes_accessed=48 << 20, transcendentals=0),
         name="own_gather",
-    )(ids, blocks, counts, feat, w_neigh, w_self)
+    )(ids, blocks, counts, feat)
 
 
 def main_kernel(
-    parts, nodes, inv_ref, near_hbm, adj_hbm, own_ref, wt_ref, wh_ref, gs_ref,
+    parts, nodes, inv_ref, near_hbm, adj_hbm, own_ref, wn_ref, ws_ref, wh_ref, gs_ref,
     scores_ref, grads_ref, head_ref,
-    near_ref, adj_ref, x_all, w_all, agg_send, head_part, head_recv, head_node, head_all,
-    g_part, g_send, g_recv, g_node,
-    w_sems, own_sems, agg_sems, hrs_sems, grs_sems, hn_sems, gn_sems, hag_sems,
+    near_ref, adj_ref, x_all, agg_send, head_part, head_sib, head_send, head_recv, head_node, head_all,
+    g_part, g_sib, g_send, g_recv, g_node,
+    pair_sems, own_sems, agg_sems, hrs_sems, grs_sems, hn_sems, gn_sems, hag_sems,
     load_sems,
 ):
     me = lax.axis_index("feat")
@@ -115,6 +111,23 @@
         return pltpu.make_async_remote_copy(
             src_ref=src, dst_ref=dst, send_sem=sems.at[0, step], recv_sem=sems.at[1, step],
             device_id={"feat": peer}, device_id_type=pl.DeviceIdType.MESH,
+        )
+
+    chips = parts // 2
+    chip, core = me // 2, lax.rem(me, 2)
+    mate = 1 - core
+
+    def chip_copy(step, src, dst, sems):
+        return pltpu.make_async_remote_copy(
+            src_ref=src, dst_ref=dst, send_sem=sems.at[0, step], recv_sem=sems.at[1, step],
+            device_id={"feat": lax.rem(chip + step, chips) * 2 + core},
+            device_id_type=pl.DeviceIdType.MESH,
+        )
+
+    def pair_copy(which, src, dst):
+        return pltpu.make_async_remote_copy(
+            src_ref=src, dst_ref=dst, send_sem=pair_sems.at[0, which], recv_sem=pair_sems.at[1, which],
+            device_id={"feat": chip * 2 + mate}, device_id_type=pl.DeviceIdType.MESH,
         )
 
     def node_copy(step, src, dst, sems):
@@ -149,15 +162,12 @@
         )
     pl.semaphore_wait(barrier, parts + nodes - 2)
 
-    w_copies, own_copies, agg_copies = [], [], []
+    own_copies, agg_copies = [], []
     for step in range(1, parts):
         peer = lax.rem(me + step, parts)
         copy = feat_copy(step, own_ref.at[peer], x_all.at[me, pl.ds(width, width)], own_sems)
         copy.start()
         own_copies.append(copy)
-        copy = feat_copy(step, wt_ref, w_all.at[me], w_sems)
-        copy.start()
-        w_copies.append(copy)
 
     def aggregate(held, tile):
         edges = jnp.concatenate([adj_ref[held, slot] for slot in range(slots)], axis=1)
@@ -178,15 +188,19 @@
             copy.start()
             agg_copies.append(copy)
     x_all[me, width:, :] = own_ref[me]
-    w_all[me] = wt_ref[...]
 
     grad_t = gs_ref[...].astype(F32).T.astype(BF16)
     head_t = wh_ref[...].astype(F32).T.astype(BF16)
     grad_hidden = nn(head_t, grad_t)
 
-    for copy in w_copies:
-        copy.wait_recv()
-    weights = w_all[...].reshape(parts * 2 * width, hid).astype(F32).T.astype(BF16)
+    weights = jnp.concatenate(
+        [
+            wn_ref[...].reshape(parts, width, hid).astype(F32),
+            ws_ref[...].reshape(parts, width, hid).astype(F32),
+        ],
+        axis=1,
+    )
+    weights = weights.reshape(parts * 2 * width, hid).T.astype(BF16)
     for copy in own_copies:
         copy.wait_recv()
     for copy in agg_copies:
@@ -196,25 +210,33 @@
     sigma = 1.0 / (1.0 + jnp.exp(-preact))
     hidden = (preact * sigma).astype(BF16)
     head_part[...] = nt(grad_t, hidden).reshape(head_part.shape)
-    hrs = []
-    for step in range(1, parts):
-        peer = lax.rem(me + step, parts)
-        copy = feat_copy(step, head_part.at[peer], head_recv.at[step], hrs_sems)
-        copy.start()
-        hrs.append(copy)
+    head_pair = pair_copy(0, head_part.at[:, mate], head_sib)
+    head_pair.start()
     grad_pre = (grad_hidden * sigma * (1.0 + preact * (1.0 - sigma))).astype(BF16)
     grads = nt(x, grad_pre).reshape(g_part.shape)
     g_part[...] = grads
-    g_send[...] = grads.astype(BF16)
+    g_pair = pair_copy(1, g_part.at[:, mate], g_sib)
+    g_pair.start()
+
+    head_pair.wait_recv()
+    hrs = []
+    for step in range(1, chips):
+        to = lax.rem(chip + step, chips)
+        head_send[step] = head_part[to, core] + head_sib[to]
+        copy = chip_copy(step, head_send.at[step], head_recv.at[step], hrs_sems)
+        copy.start()
+        hrs.append(copy)
+    g_pair.wait_recv()
     grs = []
-    for step in range(1, parts):
-        peer = lax.rem(me + step, parts)
-        copy = feat_copy(step, g_send.at[peer], g_recv.at[step], grs_sems)
+    for step in range(1, chips):
+        to = lax.rem(chip + step, chips)
+        g_send[step] = (g_part[to, core] + g_sib[to]).astype(BF16)
+        copy = chip_copy(step, g_send.at[step], g_recv.at[step], grs_sems)
         copy.start()
         grs.append(copy)
     scores_ref[...] = nn(wh_ref[...], hidden).T.astype(BF16)
 
-    total = head_part[me]
+    total = head_part[chip, core] + head_sib[chip]
     for step, copy in enumerate(hrs, 1):
         copy.wait_recv()
         total += head_recv[step]
@@ -225,7 +247,7 @@
         copy.start()
         hns.append(copy)
 
-    total = g_part[me]
+    total = g_part[chip, core] + g_sib[chip]
     for step, copy in enumerate(grs, 1):
         copy.wait_recv()
         total += g_recv[step].astype(F32)
@@ -258,11 +280,11 @@
     for copy in hags:
         copy.wait_recv()
     head_ref[...] = head_all[...].reshape(head_ref.shape)
-    for copy in (*w_copies, *own_copies, *agg_copies, *hrs, *grs, *hns, *gns, *hags):
+    for copy in (head_pair, g_pair, *own_copies, *agg_copies, *hrs, *grs, *hns, *gns, *hags):
         copy.wait_send()
 
 
-def main_call(parts, nodes, inv, near, adj, own, wt, w_head, grad_scores):
+def main_call(parts, nodes, inv, near, adj, own, wn, ws, w_head, grad_scores):
     width = near.shape[1]
     targets, out = grad_scores.shape
     hid = w_head.shape[1]
@@ -270,6 +292,8 @@
     anywhere = pl.BlockSpec(memory_space=pl.ANY)
     head_rows = out // parts
     feat_sems = pltpu.SemaphoreType.DMA((2, parts))
+    chips = parts // 2
+    chip_sems = pltpu.SemaphoreType.DMA((2, chips))
     node_sems = pltpu.SemaphoreType.DMA((2, nodes))
     return pl.pallas_call(
         functools.partial(main_kernel, parts, nodes),
@@ -278,30 +302,32 @@
             jax.ShapeDtypeStruct((2 * width, hid), F32),
             jax.ShapeDtypeStruct((out, hid), F32),
         ),
-        in_specs=[vmem, anywhere, anywhere] + [vmem] * 4,
+        in_specs=[vmem, anywhere, anywhere] + [vmem] * 5,
         out_specs=(vmem, vmem, vmem),
         scratch_shapes=[
             pltpu.VMEM(near.shape, BF16),
             pltpu.VMEM(adj.shape, BF16),
             pltpu.VMEM((parts, 2 * width, targets), BF16),
-            pltpu.VMEM((parts, 2 * width, hid), BF16),
             pltpu.VMEM((parts, width, targets), BF16),
-            pltpu.VMEM((parts, head_rows, hid), F32),
-            pltpu.VMEM((parts, head_rows, hid), F32),
+            pltpu.VMEM((chips, 2, head_rows, hid), F32),
+            pltpu.VMEM((chips, head_rows, hid), F32),
+            pltpu.VMEM((chips, head_rows, hid), F32),
+            pltpu.VMEM((chips, head_rows, hid), F32),
             pltpu.VMEM((nodes, head_rows, hid), F32),
             pltpu.VMEM((parts, head_rows, hid), F32),
-            pltpu.VMEM((parts, 2 * width, hid), F32),
-            pltpu.VMEM((parts, 2 * width, hid), BF16),
-            pltpu.VMEM((parts, 2 * width, hid), BF16),
+            pltpu.VMEM((chips, 2, 2 * width, hid), F32),
+            pltpu.VMEM((chips, 2 * width, hid), F32),
+            pltpu.VMEM((chips, 2 * width, hid), BF16),
+            pltpu.VMEM((chips, 2 * width, hid), BF16),
             pltpu.VMEM((nodes, 2 * width, hid), BF16),
-            feat_sems, feat_sems, feat_sems, feat_sems, feat_sems, node_sems, node_sems, feat_sems,
+            pltpu.SemaphoreType.DMA((2, 2)), feat_sems, feat_sems, chip_sems, chip_sems, node_sems, node_sems, feat_sems,
             pltpu.SemaphoreType.DMA((2, parts)),
         ],
         compiler_params=pltpu.CompilerParams(
             collective_id=0, has_side_effects=True, vmem_limit_bytes=VMEM_BYTES
         ),
         name="train_step",
-    )(inv, near, adj, own, wt, w_head, grad_scores)
+    )(inv, near, adj, own, wn, ws, w_head, grad_scores)
 
 
 def hand_over_kernel(scores_in, head_in, grads_in, scores_ref, head_ref, neigh_ref, self_ref):
@@ -334,11 +360,11 @@
     ):
         feat = features[0]
         counts = tile_counts[0]
-        own, near, wt, inv = gather_own(
-            target_ids[0], block_ids[0].T, counts, feat, w_neigh.T, w_self.T, parts
-        )
+        wn = lax.all_gather(w_neigh.T, "feat", axis=0, tiled=True)
+        ws = lax.all_gather(w_self.T, "feat", axis=0, tiled=True)
+        own, near, inv = gather_own(target_ids[0], block_ids[0].T, counts, feat, parts)
         scores, grads, head = main_call(
-            parts, nodes, inv, near, adjacency[0], own, wt, w_head, grad_scores[0]
+            parts, nodes, inv, near, adjacency[0], own, wn, ws, w_head, grad_scores[0]
         )
         scores, head, neigh, own_grad = hand_over(scores, head, grads)
         return scores[None], head, neigh.T, own_grad.T

time: 59.8 us -> 72.8 us (1.22)
  blocking collectives: 0 us -> 22.7 us
  Pallas kernels: 58.2 us -> 49.1 us
    all_gather x0 -> x2, blocking collectives: none -> 22.7 us  [the longest x1 12.6 us: body(): wn = lax.all_gather(w_neigh.T, 'feat', axis=0, tiled=True)]
    pallas_call x1, Pallas kernels: 43.2 us -> 34.2 us  [main_call(): pl.pallas_call(functools.partial(main_kernel, parts, nodes), out_shape=(j...]
where the time goes in v3:
time: 72.8 us; the launch traced here: 72.5 us
  Pallas kernels  49.1 us (67%)
  blocking collectives  22.7 us (31%)
    pallas_call x1, Pallas kernels, main_call(): pl.pallas_call(functools.partial(main_kernel, parts, nodes), out_shape=(j...  34.2 us
    pallas_call x1, Pallas kernels, gather_own(): pl.pallas_call(gather_kernel, out_shape=(jax.ShapeDtypeStruct((parts, wid...  13 us
    all_gather x1, blocking collectives, body(): wn = lax.all_gather(w_neigh.T, 'feat', axis=0, tiled=True)  12.6 us
    all_gather x1, blocking collectives, body(): ws = lax.all_gather(w_self.T, 'feat', axis=0, tiled=True)  10.1 us
    pallas_call x1, Pallas kernels, hand_over(): pl.pallas_call(hand_over_kernel, out_shape=(jax.ShapeDtypeStruct(scores.s...  1.91 us

profile of v3, /device:TPU:0, one launch (start us, length us, event | category | flops | bytes accessed | tf_op | source)
XLA Modules:
  0.0 72.5 jit_solution(11733316859472388362)
XLA Ops:
  0.6 12.6 %all_gather.6.wn_ref = bf16[512,256]{1,0:T(8,128)(2,1)} all-gather(bf16[64,256]{1,0:T(8,128)(2,1)} %bitcast.16), channel_id=1, replica_groups=mesh['feat'=8,'node'=4] {'feat'}, dimensions={0}, use_global_device_ids=true | all-gather | bytes 294912 | tf_op jit(solution)/shard_map/all_gather | solution.py:363
  13.2 10.1 %all_gather.7.ws_ref = bf16[512,256]{1,0:T(8,128)(2,1)} all-gather(bf16[64,256]{1,0:T(8,128)(2,1)} %bitcast.17), channel_id=1, replica_groups=mesh['feat'=8,'node'=4] {'feat'}, dimensions={0}, use_global_device_ids=true | all-gather | bytes 294912 | tf_op jit(solution)/shard_map/all_gather | solution.py:364
  23.3 13.0 %own_gather.1 = (bf16[8,64,512]{2,1,0:T(8,128)(2,1)}, bf16[32,64,1024]{2,1,0:T(8,128)(2,1)}, f32[32,128]{1,0:T(8,128)}) custom-call(s32[4096]{0:T(1024)} %bitcast.18, s32[8,32]{1,0:T(8,128)} %bitcast.19, s32[32]{0:T(128)} %bitcast.20, bf16[64,16384]{1,0:T(8,128)(2,1)} %bitcast.14), custom_call_target="tpu_custom_call" | custom-call | bytes 50331648 | tf_op jit(solution)/shard_map/own_gather/pallas_call | solution.py:72
  36.3 34.2 %train_step.1 = (bf16[512,256]{1,0:T(8,128)(2,1)}, f32[128,256]{1,0:T(8,128)}, f32[256,256]{1,0:T(8,128)}) custom-call(f32[32,128]{1,0:T(8,128)} %get-tuple-element.14.inv_ref, bf16[32,64,1024]{2,1,0:T(8,128)(2,1)} %get-tuple-element.15.near_hbm, bf16[32,8,128,128]{3,2,1,0:T(8,128)(2,1)} %bitcast.13, bf16[8,64,512]{2,1,0:T(8,128)(2,1)} %get-tuple-element.16.own_ref, ...), custom_call_target="tpu_custom_call" | custom-call | tf_op jit(solution)/shard_map/train_step/pallas_call | solution.py:298
  70.6 1.9 %hand_over.1 = (bf16[512,256]{1,0:T(8,128)(2,1)}, f32[256,256]{1,0:T(8,128)}, f32[64,256]{1,0:T(8,128)}, f32[64,256]{1,0:T(8,128)}) custom-call(bf16[512,256]{1,0:T(8,128)(2,1)} %get-tuple-element.17.scores_in, f32[256,256]{1,0:T(8,128)} %get-tuple-element.18.head_in, f32[128,256]{1,0:T(8,128)} %get-tuple-element.19.grads_in), custom_call_target="tpu_custom_call" | custom-call | tf_op jit(solution)/shard_map/hand_over/pallas_call | solution.py:344

commit v4 on v3

--- a/solution.py
+++ b/solution.py
@@ -21,11 +21,13 @@
 
 
 def gather_kernel(
-    ids_ref, blocks_ref, counts_ref, feat_ref, own_ref, near_out, inv_ref,
+    ids_ref, blocks_ref, counts_ref, feat_ref, wn_ref, ws_ref, own_ref, near_out, wt_ref, inv_ref,
     table, rows, near_ref, near_sem,
 ):
     width, sources = feat_ref.shape
     parts, _, targets = own_ref.shape
+    wt_ref[:width, :] = wn_ref[...]
+    wt_ref[width:, :] = ws_ref[...]
     tiles = near_ref.shape[0]
     slots = near_ref.shape[2] // 128
 
@@ -63,7 +65,7 @@
     near_copy.wait()
 
 
-def gather_own(ids, blocks, counts, feat, parts):
+def gather_own(ids, blocks, counts, feat, w_neigh, w_self, parts):
     width, sources = feat.shape
     targets = ids.shape[0] // parts
     slots, tiles = blocks.shape
@@ -74,10 +76,11 @@
         out_shape=(
             jax.ShapeDtypeStruct((parts, width, targets), BF16),
             jax.ShapeDtypeStruct((tiles, width, slots * 128), BF16),
+            jax.ShapeDtypeStruct((2 * width, w_neigh.shape[1]), BF16),
             jax.ShapeDtypeStruct((tiles, 128), F32),
         ),
-        in_specs=[smem, smem, smem, vmem],
-        out_specs=(vmem, pl.BlockSpec(memory_space=pl.ANY), vmem),
+        in_specs=[smem, smem, smem, vmem, vmem, vmem],
+        out_specs=(vmem, pl.BlockSpec(memory_space=pl.ANY), vmem, vmem),
         scratch_shapes=[
             pltpu.VMEM((sources, width), F32),
             pltpu.VMEM((128, width), F32),
@@ -87,15 +90,15 @@
         compiler_params=pltpu.CompilerParams(vmem_limit_bytes=VMEM_BYTES),
         cost_estimate=pl.CostEstimate(flops=0, bytes_accessed=48 << 20, transcendentals=0),
         name="own_gather",
-    )(ids, blocks, counts, feat)
+    )(ids, blocks, counts, feat, w_neigh, w_self)
 
 
 def main_kernel(
-    parts, nodes, inv_ref, near_hbm, adj_hbm, own_ref, wn_ref, ws_ref, wh_ref, gs_ref,
+    parts, nodes, inv_ref, near_hbm, adj_hbm, own_ref, wt_ref, wh_ref, gs_ref,
     scores_ref, grads_ref, head_ref,
-    near_ref, adj_ref, x_all, agg_send, head_part, head_sib, head_send, head_recv, head_node, head_all,
+    near_ref, adj_ref, x_all, w_all, agg_send, head_part, head_sib, head_send, head_recv, head_node, head_all,
     g_part, g_sib, g_send, g_recv, g_node,
-    pair_sems, own_sems, agg_sems, hrs_sems, grs_sems, hn_sems, gn_sems, hag_sems,
+    w_sems, mate_sems, pair_sems, own_sems, agg_sems, hrs_sems, grs_sems, hn_sems, gn_sems, hag_sems,
     load_sems,
 ):
     me = lax.axis_index("feat")
@@ -162,6 +165,20 @@
         )
     pl.semaphore_wait(barrier, parts + nodes - 2)
 
+    w_copies = [
+        chip_copy(step, wt_ref, w_all.at[chip, core], w_sems) for step in range(1, chips)
+    ]
+    for copy in w_copies:
+        copy.start()
+
+    def mate_copy(step, src, dst):
+        return pltpu.make_async_remote_copy(
+            src_ref=src, dst_ref=dst, send_sem=mate_sems.at[0, step], recv_sem=mate_sems.at[1, step],
+            device_id={"feat": chip * 2 + mate}, device_id_type=pl.DeviceIdType.MESH,
+        )
+
+    mates = [mate_copy(0, wt_ref, w_all.at[chip, core])]
+    mates[0].start()
     own_copies, agg_copies = [], []
     for step in range(1, parts):
         peer = lax.rem(me + step, parts)
@@ -187,20 +204,22 @@
             copy = feat_copy(step, agg_send.at[step], x_all.at[me, pl.ds(0, width)], agg_sems)
             copy.start()
             agg_copies.append(copy)
+    for step, copy in enumerate(w_copies, 1):
+        copy.wait_recv()
+        held = w_all.at[lax.rem(chip + chips - step, chips), core]
+        copy = mate_copy(step, held, held)
+        copy.start()
+        mates.append(copy)
+    w_all[chip, core] = wt_ref[...]
     x_all[me, width:, :] = own_ref[me]
 
     grad_t = gs_ref[...].astype(F32).T.astype(BF16)
     head_t = wh_ref[...].astype(F32).T.astype(BF16)
     grad_hidden = nn(head_t, grad_t)
 
-    weights = jnp.concatenate(
-        [
-            wn_ref[...].reshape(parts, width, hid).astype(F32),
-            ws_ref[...].reshape(parts, width, hid).astype(F32),
-        ],
-        axis=1,
-    )
-    weights = weights.reshape(parts * 2 * width, hid).T.astype(BF16)
+    for copy in mates:
+        copy.wait_recv()
+    weights = w_all[...].reshape(parts * 2 * width, hid).astype(F32).T.astype(BF16)
     for copy in own_copies:
         copy.wait_recv()
     for copy in agg_copies:
@@ -280,11 +299,11 @@
     for copy in hags:
         copy.wait_recv()
     head_ref[...] = head_all[...].reshape(head_ref.shape)
-    for copy in (head_pair, g_pair, *own_copies, *agg_copies, *hrs, *grs, *hns, *gns, *hags):
+    for copy in (*w_copies, *mates, head_pair, g_pair, *own_copies, *agg_copies, *hrs, *grs, *hns, *gns, *hags):
         copy.wait_send()
 
 
-def main_call(parts, nodes, inv, near, adj, own, wn, ws, w_head, grad_scores):
+def main_call(parts, nodes, inv, near, adj, own, wt, w_head, grad_scores):
     width = near.shape[1]
     targets, out = grad_scores.shape
     hid = w_head.shape[1]
@@ -302,12 +321,13 @@
             jax.ShapeDtypeStruct((2 * width, hid), F32),
             jax.ShapeDtypeStruct((out, hid), F32),
         ),
-        in_specs=[vmem, anywhere, anywhere] + [vmem] * 5,
+        in_specs=[vmem, anywhere, anywhere] + [vmem] * 4,
         out_specs=(vmem, vmem, vmem),
         scratch_shapes=[
             pltpu.VMEM(near.shape, BF16),
             pltpu.VMEM(adj.shape, BF16),
             pltpu.VMEM((parts, 2 * width, targets), BF16),
+            pltpu.VMEM((chips, 2, 2 * width, hid), BF16),
             pltpu.VMEM((parts, width, targets), BF16),
             pltpu.VMEM((chips, 2, head_rows, hid), F32),
             pltpu.VMEM((chips, head_rows, hid), F32),
@@ -320,14 +340,14 @@
             pltpu.VMEM((chips, 2 * width, hid), BF16),
             pltpu.VMEM((chips, 2 * width, hid), BF16),
             pltpu.VMEM((nodes, 2 * width, hid), BF16),
-            pltpu.SemaphoreType.DMA((2, 2)), feat_sems, feat_sems, chip_sems, chip_sems, node_sems, node_sems, feat_sems,
+            chip_sems, chip_sems, pltpu.SemaphoreType.DMA((2, 2)), feat_sems, feat_sems, chip_sems, chip_sems, node_sems, node_sems, feat_sems,
             pltpu.SemaphoreType.DMA((2, parts)),
         ],
         compiler_params=pltpu.CompilerParams(
             collective_id=0, has_side_effects=True, vmem_limit_bytes=VMEM_BYTES
         ),
         name="train_step",
-    )(inv, near, adj, own, wn, ws, w_head, grad_scores)
+    )(inv, near, adj, own, wt, w_head, grad_scores)
 
 
 def hand_over_kernel(scores_in, head_in, grads_in, scores_ref, head_ref, neigh_ref, self_ref):
@@ -360,11 +380,11 @@
     ):
         feat = features[0]
         counts = tile_counts[0]
-        wn = lax.all_gather(w_neigh.T, "feat", axis=0, tiled=True)
-        ws = lax.all_gather(w_self.T, "feat", axis=0, tiled=True)
-        own, near, inv = gather_own(target_ids[0], block_ids[0].T, counts, feat, parts)
+        own, near, wt, inv = gather_own(
+            target_ids[0], block_ids[0].T, counts, feat, w_neigh.T, w_self.T, parts
+        )
         scores, grads, head = main_call(
-            parts, nodes, inv, near, adjacency[0], own, wn, ws, w_head, grad_scores[0]
+            parts, nodes, inv, near, adjacency[0], own, wt, w_head, grad_scores[0]
         )
         scores, head, neigh, own_grad = hand_over(scores, head, grads)
         return scores[None], head, neigh.T, own_grad.T

time: 72.8 us -> 55.2 us (0.76)
  blocking collectives: 22.7 us -> 0 us
  Pallas kernels: 49.1 us -> 54.4 us
    all_gather x2 -> x0, blocking collectives: 22.7 us -> none  [the longest x1 12.6 us: body(): wn = lax.all_gather(w_neigh.T, 'feat', axis=0, tiled=True)]
    pallas_call x1, Pallas kernels: 34.2 us -> 39.4 us  [main_call(): pl.pallas_call(functools.partial(main_kernel, parts, nodes), out_shape=(j...]
where the time goes in v4:
time: 55.2 us; the launch traced here: 55 us
  Pallas kernels  54.4 us (99%)
  between operations  0.65 us (1%)
    pallas_call x1, Pallas kernels, main_call(): pl.pallas_call(functools.partial(main_kernel, parts, nodes), out_shape=(j...  39.4 us
    pallas_call x1, Pallas kernels, gather_own(): pl.pallas_call(gather_kernel, out_shape=(jax.ShapeDtypeStruct((parts, wid...  13.1 us
    pallas_call x1, Pallas kernels, hand_over(): pl.pallas_call(hand_over_kernel, out_shape=(jax.ShapeDtypeStruct(scores.s...  1.91 us

profile of v4, /device:TPU:0, one launch (start us, length us, event | category | flops | bytes accessed | tf_op | source)
XLA Modules:
  0.0 55.0 jit_solution(17791909300223894630)
XLA Ops:
  0.6 13.1 %own_gather.1 = (bf16[8,64,512]{2,1,0:T(8,128)(2,1)}, bf16[32,64,1024]{2,1,0:T(8,128)(2,1)}, bf16[128,256]{1,0:T(8,128)(2,1)}, f32[32,128]{1,0:T(8,128)}) custom-call(s32[4096]{0:T(1024)} %bitcast.18, s32[8,32]{1,0:T(8,128)} %bitcast.19, s32[32]{0:T(128)} %bitcast.20, bf16[64,16384]{1,0:T(8,128)(2,1)} %bitcast.14, bf16[64,256]{1,0:T(8,128)(2,1)} %bitcast.16, ...), custom_call_target="tpu_custom_call" | custom-call | bytes 50331648 | tf_op jit(solution)/shard_map/own_gather/pallas_call | solution.py:74
  13.7 39.4 %train_step.1 = (bf16[512,256]{1,0:T(8,128)(2,1)}, f32[128,256]{1,0:T(8,128)}, f32[256,256]{1,0:T(8,128)}) custom-call(f32[32,128]{1,0:T(8,128)} %get-tuple-element.15.inv_ref, bf16[32,64,1024]{2,1,0:T(8,128)(2,1)} %get-tuple-element.16.near_hbm, bf16[32,8,128,128]{3,2,1,0:T(8,128)(2,1)} %bitcast.13, bf16[8,64,512]{2,1,0:T(8,128)(2,1)} %get-tuple-element.17.own_ref, ...), custom_call_target="tpu_custom_call" | custom-call | tf_op jit(solution)/shard_map/train_step/pallas_call | solution.py:317
  53.1 1.9 %hand_over.1 = (bf16[512,256]{1,0:T(8,128)(2,1)}, f32[256,256]{1,0:T(8,128)}, f32[64,256]{1,0:T(8,128)}, f32[64,256]{1,0:T(8,128)}) custom-call(bf16[512,256]{1,0:T(8,128)(2,1)} %get-tuple-element.19.scores_in, f32[256,256]{1,0:T(8,128)} %get-tuple-element.20.head_in, f32[128,256]{1,0:T(8,128)} %get-tuple-element.21.grads_in), custom_call_target="tpu_custom_call" | custom-call | tf_op jit(solution)/shard_map/hand_over/pallas_call | solution.py:364
